TPU v7x, 32 devices: a whole 2x2x4 slice. The times are simulated.
32 devices in a mesh: section: 2 (over x), seq: 8 (over z, y), head: 2 (over core).
Axes of the slice: x: 2, y: 2, z: 4, core: 2. Of those that a mesh axis runs over, the one named last changes fastest.
Arguments:
- query_nope: bfloat16 [2, 1024, 64, 128], P('section', 'seq', 'head'), may hold values from -6 to 6
- query_rope: bfloat16 [2, 1024, 4096], P('section', 'seq', 'head'), may hold values from -8 to 8
- latent: bfloat16 [2, 1024, 576], P('section', ('seq', 'head')), may hold values from -8 to 8
- up_key: bfloat16 [64, 512, 128], P('head'), may hold values from -0.25 to 0.25
- value_up_weight: bfloat16 [64, 512, 128], P('head'), may hold values from -1.5 to 1.5
- lengths: int32 [4], replicated, may hold values from 1 to 640, 1024 in all
- owner_request_table: int32 [32], replicated, may hold values from 0 to 31, each once
Outputs:
- attended: bfloat16 [2, 1024, 64, 128], P('section', 'seq', 'head')
Inputs may be any that keep to these rules, and one draw needn't show every extreme that they name: The 4 lengths sum to 1024; one is exactly 640. `owner_request_table`: every request 0 to 31 appears once.
All inputs are finite; a program needn't handle non-finite values.
Results may differ from a plain program's by a relative error of at most 0.0075.
Values may be sent and summed in bfloat16 or wider, within the bound.
No kernel may reach another device: no remote copies, remote signals or barrier semaphores. Data moves between devices by JAX's collectives and lax.ppermute only.
A program may use at most 128 MiB of HBM per device.

v0:
```python
import functools
import math

import jax
import jax.numpy as jnp
from jax import lax
from jax.experimental import pallas as pl
from jax.experimental.pallas import tpu as pltpu
from jax.sharding import PartitionSpec as P

SAMPLES = 8
STEPS = 4
BLOCK = 64
KEY_TILE = 256
ALIGN = 16
LANES = 128

EARLY = ((0, 0), (0, 1), (0, 2), (1, 0))
LATE = ((1, 1), (1, 2), (0, 3), (1, 3))

scale_top = 448.0
tiny_eps = 1e-06
masked_low = -1e30


def absorb_kernel(nope_ref, rope_ref, up_ref, *rest):
    out_ref, wide = rest[-2:]
    tokens, heads, nope_dim = nope_ref.shape
    rank = up_ref.shape[1]
    rope_dim = rope_ref.shape[1] // heads
    wide[...] = nope_ref[...].astype(jnp.float32).reshape(tokens * heads, nope_dim)
    for head in range(heads):
        rows = wide[pl.ds(head, tokens, stride=heads), :].astype(jnp.bfloat16)
        lifted = lax.dot_general(
            rows, up_ref[head], (((1,), (1,)), ((), ())), preferred_element_type=jnp.float32
        )
        out_ref[head, :, :rank] = lifted.astype(jnp.bfloat16)
        rope = rope_ref[:, head * rope_dim : (head + 1) * rope_dim]
        out_ref[head, :, rank : rank + rope_dim] = rope


def absorb(query_nope, query_rope, up_key, group, first, count, prior=None):
    tokens, heads, nope_dim = query_nope.shape
    rank = up_key.shape[1]
    rope_dim = query_rope.shape[1] // heads
    at = first // group
    operands = [
        pltpu.with_memory_space_constraint(operand, pltpu.HBM)
        for operand in (query_nope, query_rope, up_key)
    ]
    in_specs = [
        pl.BlockSpec((tokens, group, nope_dim), lambda g: (0, g + at, 0)),
        pl.BlockSpec((tokens, group * rope_dim), lambda g: (0, g + at)),
        pl.BlockSpec((group, rank, nope_dim), lambda g: (g + at, 0, 0)),
    ]
    if prior is not None:
        in_specs.append(pl.BlockSpec(memory_space=pl.ANY))
        operands.append(prior)
    return pl.pallas_call(
        absorb_kernel,
        grid=(count // group,),
        in_specs=in_specs,
        out_specs=pl.BlockSpec((group, tokens, rank + rope_dim), lambda g: (g + at, 0, 0)),
        out_shape=jax.ShapeDtypeStruct((heads, tokens, rank + rope_dim), jnp.bfloat16),
        scratch_shapes=[pltpu.VMEM((tokens * group, nope_dim), jnp.float32)],
        input_output_aliases={} if prior is None else {3: 0},
        compiler_params=pltpu.CompilerParams(vmem_limit_bytes=16 << 20),
        cost_estimate=pl.CostEstimate(
            flops=2 * tokens * count * nope_dim * rank,
            bytes_accessed=2 * count * (tokens * (nope_dim + rank + 2 * rope_dim) + rank * nope_dim),
            transcendentals=0,
        ),
        name="absorb",
    )(*operands)


def requantized(*parts):
    largest = jnp.full((1, 1), 0.0, jnp.float32)
    for part in parts:
        down = jnp.max(jnp.abs(part), axis=0, keepdims=True).astype(jnp.float32)
        largest = jnp.maximum(largest, jnp.max(down, axis=1, keepdims=True))
    block_scale = ((largest + tiny_eps) / scale_top).astype(jnp.bfloat16).astype(jnp.float32)
    inverse = 1.0 / block_scale
    scaled = []
    for part in parts:
        stored = (part.astype(jnp.float32) * inverse).astype(jnp.bfloat16)
        scaled.append((stored.astype(jnp.float32) * block_scale).astype(jnp.bfloat16))
    return scaled


def packed_rope(rope):
    rows = rope.astype(jnp.float32)
    return jnp.concatenate([rows[at : at + 8, :] for at in range(0, BLOCK, 8)], axis=1)


def scaled_block(source, part, keys, rows_at):
    rank = source.shape[1]
    rope_dim = keys.shape[1] - rank
    blocks = source.shape[0] // (BLOCK + 8)
    packed = source[blocks * BLOCK :, :].astype(jnp.float32)[8 * part : 8 * part + 8, :]
    rope = jnp.concatenate(
        [packed[:, at : at + rope_dim] for at in range(0, rank, rope_dim)], axis=0
    )
    rows = source[part * BLOCK : (part + 1) * BLOCK, :]
    scaled, scaled_rope = requantized(rows, rope)
    keys[rows_at, :rank] = scaled
    keys[rows_at, rank:] = scaled_rope


def place_bands(owner, is_decode, lengths_ref, table_ref, groups, req_dev, tokens, placed):
    band = tokens // req_dev
    prompts = lengths_ref.shape[0]
    starts = []
    running = jnp.int32(0)
    for prompt in range(prompts):
        starts.append(running)
        running = running + lengths_ref[prompt]
    for slot in range(req_dev):
        prompt_of = table_ref[owner * req_dev + slot] // groups
        decode_low = jnp.int32(0)
        decode_high = jnp.int32(0)
        first = owner * tokens + slot * band
        prefill_low = jnp.int32(0)
        for prompt in range(prompts):
            ending = starts[prompt] + lengths_ref[prompt]
            decode_low = jnp.where(prompt_of == prompt, starts[prompt], decode_low)
            decode_high = jnp.where(prompt_of == prompt, ending, decode_high)
            prefill_low = jnp.where(starts[prompt] <= first, starts[prompt], prefill_low)
        low = jnp.where(is_decode, decode_low, prefill_low)
        high = jnp.where(is_decode, decode_high, first + band)
        base = (low // ALIGN) * ALIGN
        fresh_at = ((high - base + ALIGN - 1) // ALIGN) * ALIGN
        tiles = (fresh_at + jnp.where(is_decode, band, 0) + KEY_TILE - 1) // KEY_TILE
        for at, value in enumerate((tiles, base, fresh_at, decode_low, decode_high)):
            placed[slot * 5 + at] = value
    return starts


def seen(slot, spots, lines, starts, placed, owner, is_decode, tokens, band):
    step_bits = SAMPLES.bit_length() - 1
    tiles, base, fresh_at, decode_low, decode_high = (placed[slot * 5 + at] for at in range(5))
    first = owner * tokens + slot * band
    held_spot = spots + base
    row_low = jnp.zeros(spots.shape, jnp.int32)
    for start in starts:
        row_low = jnp.where(first + lines >= start, start, row_low)
    row_low = jnp.where(is_decode, decode_low, row_low)
    row_high = jnp.where(is_decode, decode_high, first + lines + 1)
    cached = (held_spot >= row_low) & (held_spot < row_high)
    fresh = spots - fresh_at
    visible_fresh = (
        (fresh >= 0)
        & (fresh < jnp.where(is_decode, band, 0))
        & (jnp.right_shift(fresh, step_bits) <= jnp.right_shift(lines, step_bits))
        & (jnp.bitwise_and(fresh ^ lines, SAMPLES - 1) == 0)
    )
    return jnp.where(cached | visible_fresh, 0.0, masked_low)


def block_spots(masks, owner, section, core, sides):
    virtual = lax.bitwise_xor(owner, section)
    for side, piece in sides:
        side_core = core if side == 0 else 1 - core
        for part, mask in enumerate(masks[piece]):
            spot = lax.bitwise_xor(virtual, mask) * 2 + side_core
            yield part, pl.ds(pl.multiple_of(spot * BLOCK, BLOCK), BLOCK)


def early_kernel(sizes, lengths_ref, table_ref, *rest):
    masks, groups, req_dev, tokens, tokens_all = sizes
    pieces, (keys, bias, placed) = rest[:-3], rest[-3:]
    band = tokens // req_dev
    section, owner, core = (lax.axis_index(name) for name in ("section", "seq", "head"))
    is_decode = section == 1
    for here, source in zip(EARLY, pieces):
        here = [here]
        for part, rows_at in block_spots(masks, owner, section, core, here):
            scaled_block(source, part, keys, rows_at)
    pad = keys.shape[0] - tokens_all
    keys[tokens_all:, :] = jnp.zeros((pad, keys.shape[1]), jnp.bfloat16)
    starts = place_bands(owner, is_decode, lengths_ref, table_ref, groups, req_dev, tokens, placed)
    span = (band, bias.shape[1])
    for slot in range(req_dev):
        slot_bias = seen(
            slot,
            lax.broadcasted_iota(jnp.int32, span, 1),
            lax.broadcasted_iota(jnp.int32, span, 0),
            starts,
            placed,
            owner,
            is_decode,
            tokens,
            band,
        )
        bias[slot] = jnp.concatenate([slot_bias] * (LANES // band), axis=0).T


def attend_kernel(sizes, query, value_up_hbm, *rest):
    masks, groups, req_dev, rank, rate, tokens_all, most_keys, group = sizes
    compact = most_keys <= 4 * KEY_TILE
    count = len(LATE) + 3 if compact else 2 * len(masks) + 2
    pieces = rest[:count]
    own_ref, other_ref, out_hbm, *scratch = rest[count:]
    keys, value_up, latent_out, spread, result_rows = scratch[:5]
    score_even, score_odd, top_even, top_odd, placed, sems = scratch[5:11]
    bands = scratch[11:]
    heads, tokens, width = query.shape
    band = tokens // req_dev
    rows = group * band
    units = req_dev * (heads // group)
    section, owner, core = (lax.axis_index(name) for name in ("section", "seq", "head"))
    is_decode = section == 1

    value_copy = pltpu.make_async_copy(value_up_hbm, value_up, sems.at[0])
    value_copy.start()
    block_copies = []
    starts = []
    if compact:
        *last, early_keys, bias, placed = pieces
        keys[...] = early_keys[...]
        for here, source in zip(LATE, last):
            here = [here]
            for part, rows_at in block_spots(masks, owner, section, core, here):
                scaled_block(source, part, keys, rows_at)
    else:
        *pieces, lengths_ref, table_ref = pieces
        for at, source in enumerate(pieces):
            here = [divmod(at, len(masks))]
            for part, rows_at in block_spots(masks, owner, section, core, here):
                block_copies.append(
                    pltpu.make_async_copy(
                        source.at[pl.ds(part * BLOCK, BLOCK), :],
                        keys.at[rows_at, :],
                        sems.at[1 + len(block_copies)],
                    )
                )
        for copy in block_copies:
            copy.start()
        pad = keys.shape[0] - tokens_all
        keys[tokens_all:, :] = jnp.zeros((pad, width), jnp.bfloat16)
        starts = place_bands(
            owner, is_decode, lengths_ref, table_ref, groups, req_dev, tokens, placed
        )

    for copy in block_copies:
        copy.wait()
    if not compact:

        def rescale(block, carry):
            at = pl.ds(pl.multiple_of(block * BLOCK, BLOCK), BLOCK)
            keys[at, :] = requantized(keys[at, :])[0]
            return carry

        lax.fori_loop(0, tokens_all // BLOCK, rescale, 0)
    def keys_of(slot):
        return bands[slot] if compact else bands[0].at[slot]

    def fresh_rows(slot):
        share = own_ref.shape[0]
        mine, part = divmod(slot * band, share)
        here = slice(part, part + band)
        return jnp.where(core == mine, own_ref[here, :], other_ref[here, :])

    def lay_band(slot, span):
        base, fresh_at = (placed[slot * 5 + at] for at in (1, 2))
        extent = -(-span // LANES) * LANES
        band_keys, band_turned = keys_of(slot), bands[req_dev + slot]
        band_keys[:extent, :] = keys[pl.ds(pl.multiple_of(base, ALIGN), extent), :]
        at = pl.ds(pl.multiple_of(fresh_at, ALIGN), band)
        band_keys[at, :] = jnp.where(is_decode, fresh_rows(slot), band_keys[at, :])
        band_turned[:, :extent] = band_keys[:extent, :rank].T

    if not compact:
        for slot in range(req_dev):
            tiles, base, fresh_at = (placed[slot * 5 + at] for at in range(3))
            band_keys = keys_of(slot)

            def copy_tile(tile, carry):
                target = pl.multiple_of(tile * KEY_TILE, KEY_TILE)
                source = pl.multiple_of(base + tile * KEY_TILE, ALIGN)
                band_keys[pl.ds(target, KEY_TILE), :] = keys[pl.ds(source, KEY_TILE), :]
                return carry

            lax.fori_loop(0, tiles, copy_tile, 0)

            @pl.when(is_decode)
            def add_fresh():
                at = pl.ds(pl.multiple_of(fresh_at, ALIGN), band)
                band_keys[at, :] = fresh_rows(slot)

    def spots_of(unit):
        if isinstance(unit, int):
            return unit % req_dev, unit // req_dev * group, unit % req_dev * band
        slot = lax.rem(unit, req_dev)
        first_head = pl.multiple_of((unit // req_dev) * group, group)
        return slot, first_head, pl.multiple_of(slot * band, band)

    def scored(unit, key_tile, bias_tile):
        slot, first_head, offset = spots_of(unit)
        asked = query[pl.ds(first_head, group), pl.ds(offset, band), :].reshape(rows, width)
        score = lax.dot_general(
            key_tile, asked, (((1,), (1,)), ((), ())), preferred_element_type=jnp.float32
        )
        return score + jnp.concatenate([bias_tile] * (rows // LANES), axis=1)

    def keep(unit, added, total):
        slot, first_head, offset = spots_of(unit)
        result = (added * (1.0 / total)).astype(jnp.bfloat16)
        latent_out[pl.ds(first_head, group), pl.ds(offset, band), :] = result.T.reshape(
            group, band, rank
        )

    def score_unit(unit, score_ref, top_ref, span):
        slot = unit % req_dev
        score = scored(unit, keys_of(slot)[:span, :], bias[slot, :span, :])
        score_ref[:span, :] = score
        top_ref[...] = jnp.max(score.reshape(span // 8, 8, rows), axis=0)

    def fold_unit(unit, score_ref, top_ref, span):
        slot = unit % req_dev
        top = jnp.max(top_ref[...], axis=0, keepdims=True)
        expo = jnp.exp2((score_ref[:span, :] - top) * rate)
        total = jnp.sum(expo, axis=0, keepdims=True)
        added = jnp.dot(
            bands[req_dev + slot][:, :span],
            expo.astype(jnp.bfloat16),
            preferred_element_type=jnp.float32,
        )
        keep(unit, added, total)

    many = spread.shape[0] // tokens
    out_copies = []
    for at in range(0, heads, many):
        here = (slice(None), pl.ds(at, many), slice(None))
        out_copies.append(
            pltpu.make_async_copy(
                result_rows.at[here], out_hbm.at[here], sems.at[1 + len(out_copies)]
            )
        )

    def project(part):
        at = part * many
        for head in range(many):
            spread[pl.ds(head, tokens, stride=many), :] = jnp.dot(
                latent_out[at + head], value_up[at + head], preferred_element_type=jnp.float32
            )
        result_rows[:, at : at + many, :] = (
            spread[...].astype(jnp.bfloat16).reshape(tokens, many, result_rows.shape[2])
        )

    def run(span):
        def score_next(unit, score_ref, top_ref):
            if unit < req_dev:
                lay_band(unit, span)
            score_unit(unit, score_ref, top_ref, span)

        score_next(0, score_even, top_even)
        for unit in range(0, units - 2, 2):
            score_next(unit + 1, score_odd, top_odd)
            fold_unit(unit, score_even, top_even, span)
            score_next(unit + 2, score_even, top_even)
            fold_unit(unit + 1, score_odd, top_odd, span)
        value_copy.wait()
        score_unit(units - 1, score_odd, top_odd, span)
        fold_unit(units - 2, score_even, top_even, span)
        project(0)
        fold_unit(units - 1, score_odd, top_odd, span)
        out_copies[0].start()
        project(1)
        out_copies[1].start()

    def run_long(unit, carry):
        slot = lax.rem(unit, req_dev)

        def step(tile, state):
            top, total, added = state
            at = pl.ds(pl.multiple_of(tile * KEY_TILE, KEY_TILE), KEY_TILE)
            key_tile = keys_of(slot)[at, :]
            area = (KEY_TILE, LANES)
            bias_tile = seen(
                slot,
                lax.broadcasted_iota(jnp.int32, area, 0) + tile * KEY_TILE,
                jnp.bitwise_and(lax.broadcasted_iota(jnp.int32, area, 1), band - 1),
                starts,
                placed,
                owner,
                is_decode,
                tokens,
                band,
            )
            score = scored(unit, key_tile, bias_tile)
            now = jnp.maximum(top, jnp.max(score, axis=0, keepdims=True))
            shrink = jnp.exp2((top - now) * rate)
            expo = jnp.exp2((score - now) * rate)
            term = jnp.dot(
                key_tile[:, :rank].T, expo.astype(jnp.bfloat16), preferred_element_type=jnp.float32
            )
            total = total * shrink + jnp.sum(expo, axis=0, keepdims=True)
            return (now, total, added * shrink + term)

        state = (
            jnp.full((1, rows), masked_low, jnp.float32),
            jnp.zeros((1, rows), jnp.float32),
            jnp.zeros((rank, rows), jnp.float32),
        )
        top, total, added = lax.fori_loop(0, placed[slot * 5], step, state)
        keep(unit, added, total)
        return carry

    if compact:
        tiles = placed[0]
        for slot in range(1, req_dev):
            tiles = jnp.maximum(tiles, placed[slot * 5])
        for count in range(1, -(-most_keys // KEY_TILE) + 1):
            span = min(count * KEY_TILE, most_keys)
            pl.when(tiles == count)(functools.partial(run, span))
    else:
        lax.fori_loop(0, units, run_long, 0)
        value_copy.wait()
        for part, copy in enumerate(out_copies):
            project(part)
            copy.start()
    for copy in out_copies:
        copy.wait()


def key_room(tokens, tokens_all, band):
    longest = tokens_all // 2 + tokens
    most_keys = -(-(longest + ALIGN + band) // BLOCK) * BLOCK
    return most_keys, -(-most_keys // KEY_TILE) * KEY_TILE


def prepare_early(lengths, table, masks, pieces, tokens, tokens_all, width):
    req_dev = table.shape[0] // (tokens_all // tokens)
    groups = table.shape[0] // lengths.shape[0]
    room = key_room(tokens, tokens_all, tokens // req_dev)[1]
    small = pl.BlockSpec(memory_space=pltpu.SMEM)
    whole = pl.BlockSpec(memory_space=pltpu.VMEM)
    return pl.pallas_call(
        functools.partial(early_kernel, (masks, groups, req_dev, tokens, tokens_all)),
        in_specs=[small] * 2 + [whole] * len(pieces),
        out_specs=[whole, whole, small],
        out_shape=[
            jax.ShapeDtypeStruct((tokens_all + room, width), jnp.bfloat16),
            jax.ShapeDtypeStruct((req_dev, room, LANES), jnp.float32),
            jax.ShapeDtypeStruct((5 * req_dev,), jnp.int32),
        ],
        compiler_params=pltpu.CompilerParams(vmem_limit_bytes=12 << 20),
        name="early",
    )(lengths, table, *pieces)


def attend(
    lengths, table, queries, value_up, pieces, masks, own, other, tokens_all, nope_dim
):
    heads, tokens, width = queries.shape
    rank, v_dim = value_up.shape[1:]
    owners = tokens_all // tokens
    req_dev = table.shape[0] // owners
    groups = table.shape[0] // lengths.shape[0]
    band = tokens // req_dev
    longest = tokens_all // 2 + tokens
    most_keys, room = key_room(tokens, tokens_all, band)
    compact = most_keys <= 4 * KEY_TILE
    rate = math.log2(math.e) / math.sqrt(nope_dim + width - rank)
    group = 16
    many = heads // 2
    rows = group * band
    sizes = (masks, groups, req_dev, rank, rate, tokens_all, most_keys, group)
    small = pl.BlockSpec(memory_space=pltpu.SMEM)
    left = pl.BlockSpec(memory_space=pl.ANY)
    whole = pl.BlockSpec(memory_space=pltpu.VMEM)
    score = pltpu.VMEM((room if compact else KEY_TILE, rows), jnp.float32)
    top = pltpu.VMEM((8, rows), jnp.float32)
    if compact:
        bands = [pltpu.VMEM((room, width), jnp.bfloat16)] * req_dev
        bands += [pltpu.VMEM((rank, room), jnp.bfloat16)] * req_dev
    else:
        bands = [pltpu.VMEM((req_dev, room, width), jnp.bfloat16)]
        pieces = [*pieces, lengths, table]
    piece_specs = [whole] * (len(LATE) + 2) + [small] if compact else [left] * (len(pieces) - 2) + [small] * 2
    return pl.pallas_call(
        functools.partial(attend_kernel, sizes),
        in_specs=[whole, left] + piece_specs + [whole] * 2,
        out_specs=left,
        out_shape=jax.ShapeDtypeStruct((tokens, heads, v_dim), jnp.bfloat16),
        scratch_shapes=[
            pltpu.VMEM((tokens_all + (room if compact else 4 * KEY_TILE), width), jnp.bfloat16),
            pltpu.VMEM(value_up.shape, jnp.bfloat16),
            pltpu.VMEM((heads, tokens, rank), jnp.bfloat16),
            pltpu.VMEM((tokens * many, v_dim), jnp.float32),
            pltpu.VMEM((tokens, heads, v_dim), jnp.bfloat16),
            score,
            score,
            top,
            top,
            pltpu.SMEM((5 * req_dev,), jnp.int32),
            pltpu.SemaphoreType.DMA((1 + 2 * owners,)),
            *bands,
        ],
        compiler_params=pltpu.CompilerParams(vmem_limit_bytes=(36 if compact else 59) << 20),
        cost_estimate=pl.CostEstimate(
            flops=4 * heads * tokens * longest * width,
            bytes_accessed=2 * (value_up.size + heads * tokens * (width + v_dim)),
            transcendentals=heads * tokens * longest,
        ),
        name="attend",
    )(
        queries,
        pltpu.with_memory_space_constraint(value_up, pltpu.HBM),
        *pieces,
        own,
        other,
    )


def copy_kernel(source, target):
    target[...] = source[...]


def choose_kernel(own, handed, target):
    is_prefill = lax.axis_index("section") == 0
    rank = target.shape[1]

    def keep(source):
        if target.shape == source.shape:
            target[...] = source[...]
        else:
            target[:BLOCK, :] = source[:, :rank]
            target[BLOCK:, :] = packed_rope(source[:, rank:]).astype(jnp.bfloat16)

    pl.when(is_prefill)(functools.partial(keep, own))
    pl.when(jnp.logical_not(is_prefill))(functools.partial(keep, handed))


def join_kernel(first, second, target):
    if first.shape[0] % (BLOCK + 8):
        rows = first.shape[0]
        target[:rows, :] = first[...]
        target[rows:, :] = second[...]
    else:
        rows = first.shape[0] // (BLOCK + 8) * BLOCK
        target[:rows, :] = first[:rows, :]
        target[rows : 2 * rows, :] = second[:rows, :]
        ropes = [source[rows:, :].astype(jnp.float32) for source in (first, second)]
        target[2 * rows :, :] = jnp.concatenate(ropes, axis=0).astype(jnp.bfloat16)


def in_vmem(kernel, shape, *arrays):
    whole = pl.BlockSpec(memory_space=pltpu.VMEM)
    return pl.pallas_call(
        kernel,
        in_specs=[whole] * len(arrays),
        out_specs=whole,
        out_shape=jax.ShapeDtypeStruct(shape, arrays[0].dtype),
        compiler_params=pltpu.CompilerParams(vmem_limit_bytes=8 << 20),
        name="hold",
    )(*arrays)


def gathered(latent, absorb_part, early_part, rank):
    owners = lax.axis_size("seq")
    flip = lambda bit: [(owner, owner ^ bit) for owner in range(owners)]
    over = lambda chosen, bit: tuple(mask | bit for mask in chosen)
    swap = [(0, 1), (1, 0)]
    beside = lambda part, arrays, prior: lax.optimization_barrier((arrays, absorb_part(part, prior)))
    handed = lax.ppermute(
        latent, ("section", "seq"), [(owner, owners + (owner ^ 1)) for owner in range(owners)]
    )
    fresh = lax.ppermute(latent, "head", swap)
    block = latent.shape[0]
    own = in_vmem(copy_kernel, latent.shape, latent)
    handed, fresh, own = lax.optimization_barrier((handed, fresh, own))
    shape = latent.shape if early_part is None else (block + 8, rank)
    held = in_vmem(choose_kernel, shape, own, handed)
    masks = (0,)
    bit = owners // 2
    queries = None
    while bit > 2:
        received = lax.ppermute(held, "seq", flip(bit))
        if queries is None:
            received, queries = beside(0, received, None)
        held = in_vmem(join_kernel, (2 * held.shape[0], held.shape[1]), held, received)
        masks = masks + over(masks, bit)
        bit //= 2
    received = lax.ppermute(held, "seq", flip(2))
    swapped = lax.ppermute(held, "section", swap)
    held_other = lax.ppermute(held, "head", swap)
    received, queries = beside(1, received, queries)
    crossed = lax.ppermute(received, "seq", flip(1))
    received_other = lax.ppermute(received, "head", swap)
    swapped_other = lax.ppermute(swapped, "head", swap)
    later = over(masks, 2)
    all_masks = (masks, later, over(masks, 1), over(later, 1))
    prepared = ()
    if early_part is not None:
        ready = [held, received, swapped, held_other]
        crossed, prepared = lax.optimization_barrier((crossed, early_part(all_masks, ready)))
    crossed_other = lax.ppermute(crossed, "head", swap)
    if early_part is not None:
        pieces = [received_other, swapped_other, crossed, crossed_other, *prepared]
    else:
        pieces = [held, received, swapped, crossed]
        pieces += [held_other, received_other, swapped_other, crossed_other]
    return pieces, all_masks, queries, fresh


def shards(query_nope, query_rope, latent, up_key, value_up_weight, lengths, owner_request_table):
    tokens_all = lax.axis_size("seq") * query_nope.shape[1]
    own = latent[0]
    share = query_nope.shape[2] // 2

    def absorb_part(part, prior):
        return absorb(query_nope[0], query_rope[0], up_key, 8, part * share, share, prior)

    def early_part(masks, pieces):
        tokens, width = query_nope.shape[1], latent.shape[2]
        return prepare_early(
            lengths, owner_request_table, masks, pieces, tokens, tokens_all, width
        )

    compact = tokens_all <= 16 * BLOCK
    pieces, masks, queries, other = gathered(
        own, absorb_part, early_part if compact else None, up_key.shape[1]
    )
    attended = attend(
        lengths,
        owner_request_table,
        queries,
        value_up_weight,
        pieces,
        masks,
        own,
        other,
        tokens_all,
        query_nope.shape[3],
    )
    return attended[None]


def solution(mesh):
    in_specs = (
        P("section", "seq", "head", None),
        P("section", "seq", "head"),
        P("section", ("seq", "head"), None),
        P("head", None, None),
        P("head", None, None),
        P(),
        P(),
    )
    out_specs = P("section", "seq", "head", None)
    return jax.shard_map(shards, mesh=mesh, in_specs=in_specs, out_specs=out_specs, check_vma=False)
```

profile of v0, /device:TPU:21, one launch (start us, length us, event | category | flops | bytes accessed | tf_op | source)
XLA Modules:
  0.0 39.8 jit_solution(11529516132660264966)
XLA Ops:
  0.0 3.1 %collective-permute-start = (bf16[64,576]{1,0:T(8,128)(2,1)}, bf16[64,576]{1,0:T(8,128)(2,1)S(1)}, u32[]{:S(2)}, u32[]{:S(2)}) collective-permute-start(bf16[64,576]{1,0:T(8,128)(2,1)} %bitcast.4), channel_id=1, source_target_pairs={{0,18},{2,16},{4,22},{6,20},{8,26},{10,24},{12,30},{14,28},{1,19},... | collective-permute-start | bytes 221192 | tf_op jit(solution)/shard_map/ppermute | solution.py:567
  3.1 1.0 %collective-permute-start.1 = (bf16[64,576]{1,0:T(8,128)(2,1)}, bf16[64,576]{1,0:T(8,128)(2,1)S(1)}, u32[]{:S(2)}, u32[]{:S(2)}) collective-permute-start(bf16[64,576]{1,0:T(8,128)(2,1)} %bitcast.5), channel_id=1, source_target_pairs={{0,1},{1,0},{2,3},{3,2},{4,5},{5,4},{6,7},{7,6},{8,9},{9,8},{10,11... | collective-permute-start | bytes 221192 | tf_op jit(solution)/shard_map/ppermute | solution.py:570
  4.1 0.9 %copy-done = bf16[1,64,576]{2,1,0:T(8,128)(2,1)S(1)} copy-done((bf16[1,64,576]{2,1,0:T(8,128)(2,1)S(1)}, bf16[1,64,576]{2,1,0:T(8,128)(2,1)}, u32[]{:S(2)}) %copy-start) | copy-done | bytes 73752
  5.0 0.0 collective-permute-done.handed
  5.0 0.2 collective-permute-done.1.rest_8_
  5.2 0.1 hold.4.first
  5.3 0.1 collective-permute-start.2
  5.4 2.4 %absorb.2.rest_0_ = bf16[32,128,576]{2,1,0:T(8,128)(2,1)S(1)} custom-call(bf16[128,32,128]{2,1,0:T(8,128)(2,1)} %bitcast.8, bf16[128,2048]{1,0:T(8,128)(2,1)} %bitcast.10, bf16[32,512,128]{2,1,0:T(8,128)(2,1)} %up_ref.3), custom_call_target="tpu_custom_call" | custom-call | flops 268435456 | bytes 5242880 | tf_op jit(solution)/shard_map/absorb/pallas_call | solution.py:59
  7.8 1.7 %collective-permute-done.2.second = bf16[72,512]{1,0:T(8,128)(2,1)S(1)} collective-permute-done((bf16[72,512]{1,0:T(8,128)(2,1)S(1)}, bf16[72,512]{1,0:T(8,128)(2,1)S(1)}, u32[]{:S(2)}, u32[]{:S(2)}) %collective-permute-start.2) | collective-permute-done | bytes 73760 | tf_op jit(solution)/shard_map/ppermute | solution.py:580
  9.5 0.0 copy-start.2
  9.5 0.0 copy-start.3
  9.5 0.0 copy-start.1
  9.5 2.0 %collective-permute-start.3 = (bf16[144,512]{1,0:T(8,128)(2,1)S(1)}, bf16[144,512]{1,0:T(8,128)(2,1)S(1)}, u32[]{:S(2)}, u32[]{:S(2)}) collective-permute-start(bf16[144,512]{1,0:T(8,128)(2,1)S(1)} %hold.5.rest_0_), channel_id=1, source_target_pairs={{0,4},{2,6},{4,0},{6,2},{8,12},{10,14},{12,8},{14,10},{1,5},{3,7},... | collective-permute-start | bytes 442376 | tf_op jit(solution)/shard_map/ppermute | solution.py:586
  11.5 2.3 %collective-permute-start.5 = (bf16[144,512]{1,0:T(8,128)(2,1)S(1)}, bf16[144,512]{1,0:T(8,128)(2,1)S(1)}, u32[]{:S(2)}, u32[]{:S(2)}) collective-permute-start(bf16[144,512]{1,0:T(8,128)(2,1)S(1)} %hold.5.rest_0_), channel_id=1, source_target_pairs={{0,16},{16,0},{1,17},{17,1},{2,18},{18,2},{3,19},{19,3},{4,20},{20... | collective-permute-start | bytes 442376 | tf_op jit(solution)/shard_map/ppermute | solution.py:587
  13.8 3.5 %collective-permute-start.8 = (bf16[144,512]{1,0:T(8,128)(2,1)S(1)}, bf16[144,512]{1,0:T(8,128)(2,1)S(1)}, u32[]{:S(2)}, u32[]{:S(2)}) collective-permute-start(bf16[144,512]{1,0:T(8,128)(2,1)S(1)} %hold.5.rest_0_), channel_id=1, source_target_pairs={{0,1},{1,0},{2,3},{3,2},{4,5},{5,4},{6,7},{7,6},{8,9},{9,8},{10,11... | collective-permute-start | bytes 442376 | tf_op jit(solution)/shard_map/ppermute | solution.py:588
  17.3 2.4 %absorb.3.query = bf16[32,128,576]{2,1,0:T(8,128)(2,1)S(1)} custom-call(bf16[128,32,128]{2,1,0:T(8,128)(2,1)} %bitcast.9, bf16[128,2048]{1,0:T(8,128)(2,1)} %bitcast.11, bf16[32,512,128]{2,1,0:T(8,128)(2,1)} %up_ref.3, bf16[32,128,576]{2,1,0:T(8,128)(2,1)S(1)} %absorb.2.rest_0_), custom_call_target="tpu_custom_call", output_to_operand_aliasing={{}: (3, {})} | custom-call | flops 268435456 | bytes 5242880 | tf_op jit(solution)/shard_map/absorb/pallas_call | solution.py:59
  19.7 0.0 collective-permute-done.3.rest_1_
  19.7 0.3 collective-permute-start.7
  20.0 0.3 collective-permute-start.4
  20.3 0.0 collective-permute-done.5.rest_2_
  20.3 0.2 collective-permute-start.6
  20.5 0.0 collective-permute-done.8.rest_3_
  20.5 0.0 copy-done.2
  20.5 0.0 copy-done.3
  20.5 2.1 %early.1 = (bf16[1792,576]{1,0:T(8,128)(2,1)S(1)}, f32[4,768,128]{2,1,0:T(8,128)S(1)}, s32[20]{0:T(128)S(1)}) custom-call(s32[4]{0:T(128)S(1)} %copy-done.2, s32[32]{0:T(128)S(1)} %copy-done.3, bf16[144,512]{1,0:T(8,128)(2,1)S(1)} %hold.5.rest_0_, bf16[144,512]{1,0:T(8,128)(2,1)S(1)} %collective-permute-done.3.rest_1_, ...), custom_call_target="tpu_custom_call" | custom-call | tf_op jit(solution)/shard_map/early/pallas_call | solution.py:439
  22.7 2.6 %collective-permute-done.7.rest_2_ = bf16[144,512]{1,0:T(8,128)(2,1)S(1)} collective-permute-done((bf16[144,512]{1,0:T(8,128)(2,1)S(1)}, bf16[144,512]{1,0:T(8,128)(2,1)S(1)}, u32[]{:S(2)}, u32[]{:S(2)}) %collective-permute-start.7) | collective-permute-done | bytes 147488 | tf_op jit(solution)/shard_map/ppermute | solution.py:590
  25.3 0.8 %collective-permute-start.9 = (bf16[144,512]{1,0:T(8,128)(2,1)S(1)}, bf16[144,512]{1,0:T(8,128)(2,1)S(1)}, u32[]{:S(2)}, u32[]{:S(2)}) collective-permute-start(bf16[144,512]{1,0:T(8,128)(2,1)S(1)} %collective-permute-done.7.rest_2_), channel_id=1, source_target_pairs={{0,1},{1,0},{2,3},{3,2},{4,5},{5,4},{6,7},{7,6},{8,9},{9,8},{10,11... | collective-permute-start | bytes 442376 | tf_op jit(solution)/shard_map/ppermute | solution.py:599
  26.0 0.0 collective-permute-done.4.rest_0_
  26.0 0.0 collective-permute-done.6.rest_1_
  26.1 1.0 %collective-permute-done.9.rest_3_ = bf16[144,512]{1,0:T(8,128)(2,1)S(1)} collective-permute-done((bf16[144,512]{1,0:T(8,128)(2,1)S(1)}, bf16[144,512]{1,0:T(8,128)(2,1)S(1)}, u32[]{:S(2)}, u32[]{:S(2)}) %collective-permute-start.9) | collective-permute-done | bytes 147488 | tf_op jit(solution)/shard_map/ppermute | solution.py:599
  27.1 0.0 copy-done.1
  27.1 12.6 %attend.1 = bf16[128,32,128]{2,1,0:T(8,128)(2,1)} custom-call(bf16[32,128,576]{2,1,0:T(8,128)(2,1)S(1)} %absorb.3.query, bf16[32,512,128]{2,1,0:T(8,128)(2,1)} %value_up_hbm.1, bf16[144,512]{1,0:T(8,128)(2,1)S(1)} %collective-permute-done.4.rest_0_, bf16[144,512]{1,0:T(8,128)(2,1)S(1)} %collective-permute-done.6.rest_1_, ...), custom_call_target="tpu_custom_call" | custom-call | flops 6039797760 | bytes 9961472 | tf_op jit(solution)/shard_map/attend/pallas_call | solution.py:482
  (3 shorter events, 0.0 us)
Async XLA Ops:
  0.0 5.0 %collective-permute-start = (bf16[64,576]{1,0:T(8,128)(2,1)}, bf16[64,576]{1,0:T(8,128)(2,1)S(1)}, u32[]{:S(2)}, u32[]{:S(2)}) collective-permute-start(bf16[64,576]{1,0:T(8,128)(2,1)} %bitcast.4), channel_id=1, source_target_pairs={{0,18},{2,16},{4,22},{6,20},{8,26},{10,24},{12,30},{14,28},{1,19},... | collective-permute-start | bytes 221192 | tf_op jit(solution)/shard_map/ppermute | solution.py:567
  3.1 2.2 %collective-permute-start.1 = (bf16[64,576]{1,0:T(8,128)(2,1)}, bf16[64,576]{1,0:T(8,128)(2,1)S(1)}, u32[]{:S(2)}, u32[]{:S(2)}) collective-permute-start(bf16[64,576]{1,0:T(8,128)(2,1)} %bitcast.5), channel_id=1, source_target_pairs={{0,1},{1,0},{2,3},{3,2},{4,5},{5,4},{6,7},{7,6},{8,9},{9,8},{10,11... | collective-permute-start | bytes 221192 | tf_op jit(solution)/shard_map/ppermute | solution.py:570
  4.1 0.9 %copy-start = (bf16[1,64,576]{2,1,0:T(8,128)(2,1)S(1)}, bf16[1,64,576]{2,1,0:T(8,128)(2,1)}, u32[]{:S(2)}) copy-start(bf16[1,64,576]{2,1,0:T(8,128)(2,1)} %param.9) | copy-start | bytes 221188
  5.3 4.2 %collective-permute-start.2 = (bf16[72,512]{1,0:T(8,128)(2,1)S(1)}, bf16[72,512]{1,0:T(8,128)(2,1)S(1)}, u32[]{:S(2)}, u32[]{:S(2)}) collective-permute-start(bf16[72,512]{1,0:T(8,128)(2,1)S(1)} %hold.4.first), channel_id=1, source_target_pairs={{0,8},{2,10},{4,12},{6,14},{8,0},{10,2},{12,4},{14,6},{1,9},{3,11}... | collective-permute-start | bytes 221192 | tf_op jit(solution)/shard_map/ppermute | solution.py:580
  9.5 11.0 %copy-start.2 = (s32[4]{0:T(128)S(1)}, s32[4]{0:T(128)}, u32[]{:S(2)}) copy-start(s32[4]{0:T(128)} %lengths_ref.1) | copy-start | bytes 52
  9.5 11.0 %copy-start.3 = (s32[32]{0:T(128)S(1)}, s32[32]{0:T(128)}, u32[]{:S(2)}) copy-start(s32[32]{0:T(128)} %table_ref.1) | copy-start | bytes 388
  9.5 17.5 %copy-start.1 = (bf16[1,64,576]{2,1,0:T(8,128)(2,1)S(1)}, bf16[1,64,576]{2,1,0:T(8,128)(2,1)}, u32[]{:S(2)}) copy-start(bf16[1,64,576]{2,1,0:T(8,128)(2,1)} %param.9) | copy-start | bytes 221188
  9.5 10.2 %collective-permute-start.3 = (bf16[144,512]{1,0:T(8,128)(2,1)S(1)}, bf16[144,512]{1,0:T(8,128)(2,1)S(1)}, u32[]{:S(2)}, u32[]{:S(2)}) collective-permute-start(bf16[144,512]{1,0:T(8,128)(2,1)S(1)} %hold.5.rest_0_), channel_id=1, source_target_pairs={{0,4},{2,6},{4,0},{6,2},{8,12},{10,14},{12,8},{14,10},{1,5},{3,7},... | collective-permute-start | bytes 442376 | tf_op jit(solution)/shard_map/ppermute | solution.py:586
  11.5 8.8 %collective-permute-start.5 = (bf16[144,512]{1,0:T(8,128)(2,1)S(1)}, bf16[144,512]{1,0:T(8,128)(2,1)S(1)}, u32[]{:S(2)}, u32[]{:S(2)}) collective-permute-start(bf16[144,512]{1,0:T(8,128)(2,1)S(1)} %hold.5.rest_0_), channel_id=1, source_target_pairs={{0,16},{16,0},{1,17},{17,1},{2,18},{18,2},{3,19},{19,3},{4,20},{20... | collective-permute-start | bytes 442376 | tf_op jit(solution)/shard_map/ppermute | solution.py:587
  13.8 6.8 %collective-permute-start.8 = (bf16[144,512]{1,0:T(8,128)(2,1)S(1)}, bf16[144,512]{1,0:T(8,128)(2,1)S(1)}, u32[]{:S(2)}, u32[]{:S(2)}) collective-permute-start(bf16[144,512]{1,0:T(8,128)(2,1)S(1)} %hold.5.rest_0_), channel_id=1, source_target_pairs={{0,1},{1,0},{2,3},{3,2},{4,5},{5,4},{6,7},{7,6},{8,9},{9,8},{10,11... | collective-permute-start | bytes 442376 | tf_op jit(solution)/shard_map/ppermute | solution.py:588
  19.7 5.5 %collective-permute-start.7 = (bf16[144,512]{1,0:T(8,128)(2,1)S(1)}, bf16[144,512]{1,0:T(8,128)(2,1)S(1)}, u32[]{:S(2)}, u32[]{:S(2)}) collective-permute-start(bf16[144,512]{1,0:T(8,128)(2,1)S(1)} %collective-permute-done.3.rest_1_), channel_id=1, source_target_pairs={{0,2},{2,0},{4,6},{6,4},{8,10},{10,8},{12,14},{14,12},{1,3},{3,1},... | collective-permute-start | bytes 442376 | tf_op jit(solution)/shard_map/ppermute | solution.py:590
  20.0 6.0 %collective-permute-start.4 = (bf16[144,512]{1,0:T(8,128)(2,1)S(1)}, bf16[144,512]{1,0:T(8,128)(2,1)S(1)}, u32[]{:S(2)}, u32[]{:S(2)}) collective-permute-start(bf16[144,512]{1,0:T(8,128)(2,1)S(1)} %collective-permute-done.3.rest_1_), channel_id=1, source_target_pairs={{0,1},{1,0},{2,3},{3,2},{4,5},{5,4},{6,7},{7,6},{8,9},{9,8},{10,11... | collective-permute-start | bytes 442376 | tf_op jit(solution)/shard_map/ppermute | solution.py:591
  20.3 5.8 %collective-permute-start.6 = (bf16[144,512]{1,0:T(8,128)(2,1)S(1)}, bf16[144,512]{1,0:T(8,128)(2,1)S(1)}, u32[]{:S(2)}, u32[]{:S(2)}) collective-permute-start(bf16[144,512]{1,0:T(8,128)(2,1)S(1)} %collective-permute-done.5.rest_2_), channel_id=1, source_target_pairs={{0,1},{1,0},{2,3},{3,2},{4,5},{5,4},{6,7},{7,6},{8,9},{9,8},{10,11... | collective-permute-start | bytes 442376 | tf_op jit(solution)/shard_map/ppermute | solution.py:592
  25.3 1.8 %collective-permute-start.9 = (bf16[144,512]{1,0:T(8,128)(2,1)S(1)}, bf16[144,512]{1,0:T(8,128)(2,1)S(1)}, u32[]{:S(2)}, u32[]{:S(2)}) collective-permute-start(bf16[144,512]{1,0:T(8,128)(2,1)S(1)} %collective-permute-done.7.rest_2_), channel_id=1, source_target_pairs={{0,1},{1,0},{2,3},{3,2},{4,5},{5,4},{6,7},{7,6},{8,9},{9,8},{10,11... | collective-permute-start | bytes 442376 | tf_op jit(solution)/shard_map/ppermute | solution.py:599
where the time goes:
time: 40 us; the launch traced here: 39.8 us
  Pallas kernels  19.6 us (49%)
  starting transfers between devices  13.5 us (34%)
  waiting for transfers between devices  5.54 us (14%)
  local copies, waits for them, and re-layouts  0.91 us (2%)
    pallas_call x1, Pallas kernels, attend(): pl.pallas_call(functools.partial(attend_kernel, sizes), in_specs=[whole,...  12.6 us
    pallas_call x2, Pallas kernels, absorb(): pl.pallas_call(absorb_kernel, grid=(count // group,), in_specs=in_specs,...  4.78 us
    ppermute x1, starting transfers between devices, gathered(): held_other = lax.ppermute(held, 'head', swap)  3.53 us
    ppermute x1, starting transfers between devices, gathered(): lax.ppermute(latent, ('section', 'seq'), [(owner, owners + (owner ^ 1)) f...  3.05 us
    ppermute x1, waiting for transfers between devices, gathered(): crossed = lax.ppermute(received, 'seq', flip(1))  2.58 us
    ppermute x1, starting transfers between devices, gathered(): swapped = lax.ppermute(held, 'section', swap)  2.28 us
    pallas_call x1, Pallas kernels, prepare_early(): pl.pallas_call(functools.partial(early_kernel, (masks, groups, req_dev, t...  2.13 us
    ppermute x1, starting transfers between devices, gathered(): received = lax.ppermute(held, 'seq', flip(2))  1.97 us
  transfers between devices with their start and end apart: 10, of which 4 were waited for; matrix products, arithmetic and copies ran while one was open for 0% of the time, Pallas kernels for 17%

commit v1 on v0

--- a/solution.py
+++ b/solution.py
@@ -338,14 +338,17 @@
             )
         )
 
-    def project(part):
+    def project(part, first=0, last=tokens):
         at = part * many
         for head in range(many):
-            spread[pl.ds(head, tokens, stride=many), :] = jnp.dot(
-                latent_out[at + head], value_up[at + head], preferred_element_type=jnp.float32
+            spread[pl.ds(first * many + head, last - first, stride=many), :] = jnp.dot(
+                latent_out[at + head, first:last, :],
+                value_up[at + head],
+                preferred_element_type=jnp.float32,
             )
-        result_rows[:, at : at + many, :] = (
-            spread[...].astype(jnp.bfloat16).reshape(tokens, many, result_rows.shape[2])
+        done = spread[first * many : last * many, :].astype(jnp.bfloat16)
+        result_rows[first:last, at : at + many, :] = done.reshape(
+            last - first, many, result_rows.shape[2]
         )
 
     def run(span):
@@ -358,15 +361,18 @@
         for unit in range(0, units - 2, 2):
             score_next(unit + 1, score_odd, top_odd)
             fold_unit(unit, score_even, top_even, span)
+            if unit == req_dev:
+                project(0)
             score_next(unit + 2, score_even, top_even)
             fold_unit(unit + 1, score_odd, top_odd, span)
-        value_copy.wait()
+            if unit == 0:
+                value_copy.wait()
         score_unit(units - 1, score_odd, top_odd, span)
         fold_unit(units - 2, score_even, top_even, span)
-        project(0)
+        project(1, 0, tokens - band)
         fold_unit(units - 1, score_odd, top_odd, span)
         out_copies[0].start()
-        project(1)
+        project(1, tokens - band, tokens)
         out_copies[1].start()
 
     def run_long(unit, carry):

time: 40 us -> 39.1 us (0.978)
  the two profiles are of different devices: /device:TPU:21 before, /device:TPU:19 now
where the time goes in v1:
time: 39.1 us; the launch traced here: 38.9 us
  Pallas kernels  20.1 us (51%)
  starting transfers between devices  11.5 us (29%)
  waiting for transfers between devices  6.1 us (16%)
  local copies, waits for them, and re-layouts  0.91 us (2%)
    pallas_call x1, Pallas kernels, attend(): pl.pallas_call(functools.partial(attend_kernel, sizes), in_specs=[whole,...  13.1 us
    pallas_call x2, Pallas kernels, absorb(): pl.pallas_call(absorb_kernel, grid=(count // group,), in_specs=in_specs,...  4.78 us
    ppermute x1, waiting for transfers between devices, gathered(): lax.ppermute(latent, ('section', 'seq'), [(owner, owners + (owner ^ 1)) f...  3.36 us
    ppermute x1, starting transfers between devices, gathered(): held_other = lax.ppermute(held, 'head', swap)  3.06 us
    pallas_call x1, Pallas kernels, prepare_early(): pl.pallas_call(functools.partial(early_kernel, (masks, groups, req_dev, t...  2.13 us
    ppermute x1, starting transfers between devices, gathered(): received = lax.ppermute(held, 'seq', flip(2))  1.97 us
    ppermute x1, waiting for transfers between devices, gathered(): received = lax.ppermute(held, 'seq', flip(bit))  1.72 us
    ppermute x1, starting transfers between devices, gathered(): crossed_other = lax.ppermute(crossed, 'head', swap)  1.44 us
  transfers between devices with their start and end apart: 10, of which 3 were waited for; matrix products, arithmetic and copies ran while one was open for 0% of the time, Pallas kernels for 18%

profile of v1, /device:TPU:19, one launch (start us, length us, event | category | flops | bytes accessed | tf_op | source)
XLA Modules:
  0.0 38.9 jit_solution(17942360577094927834)
XLA Ops:
  0.0 1.3 %collective-permute-start = (bf16[64,576]{1,0:T(8,128)(2,1)}, bf16[64,576]{1,0:T(8,128)(2,1)S(1)}, u32[]{:S(2)}, u32[]{:S(2)}) collective-permute-start(bf16[64,576]{1,0:T(8,128)(2,1)} %bitcast.4), channel_id=1, source_target_pairs={{0,18},{2,16},{4,22},{6,20},{8,26},{10,24},{12,30},{14,28},{1,19},... | collective-permute-start | bytes 221192 | tf_op jit(solution)/shard_map/ppermute | solution.py:573
  1.3 0.7 %collective-permute-start.1 = (bf16[64,576]{1,0:T(8,128)(2,1)}, bf16[64,576]{1,0:T(8,128)(2,1)S(1)}, u32[]{:S(2)}, u32[]{:S(2)}) collective-permute-start(bf16[64,576]{1,0:T(8,128)(2,1)} %bitcast.5), channel_id=1, source_target_pairs={{0,1},{1,0},{2,3},{3,2},{4,5},{5,4},{6,7},{7,6},{8,9},{9,8},{10,11... | collective-permute-start | bytes 221192 | tf_op jit(solution)/shard_map/ppermute | solution.py:576
  2.0 0.9 %copy-done = bf16[1,64,576]{2,1,0:T(8,128)(2,1)S(1)} copy-done((bf16[1,64,576]{2,1,0:T(8,128)(2,1)S(1)}, bf16[1,64,576]{2,1,0:T(8,128)(2,1)}, u32[]{:S(2)}) %copy-start) | copy-done | bytes 73752
  2.9 3.4 %collective-permute-done.handed = bf16[64,576]{1,0:T(8,128)(2,1)S(1)} collective-permute-done((bf16[64,576]{1,0:T(8,128)(2,1)}, bf16[64,576]{1,0:T(8,128)(2,1)S(1)}, u32[]{:S(2)}, u32[]{:S(2)}) %collective-permute-start) | collective-permute-done | bytes 73760 | tf_op jit(solution)/shard_map/ppermute | solution.py:573
  6.3 0.0 collective-permute-done.1.rest_8_
  6.3 0.1 hold.4.first
  6.4 0.1 collective-permute-start.2
  6.4 2.4 %absorb.2.rest_0_ = bf16[32,128,576]{2,1,0:T(8,128)(2,1)S(1)} custom-call(bf16[128,32,128]{2,1,0:T(8,128)(2,1)} %bitcast.8, bf16[128,2048]{1,0:T(8,128)(2,1)} %bitcast.10, bf16[32,512,128]{2,1,0:T(8,128)(2,1)} %up_ref.3), custom_call_target="tpu_custom_call" | custom-call | flops 268435456 | bytes 5242880 | tf_op jit(solution)/shard_map/absorb/pallas_call | solution.py:59
  8.8 1.7 %collective-permute-done.2.second = bf16[72,512]{1,0:T(8,128)(2,1)S(1)} collective-permute-done((bf16[72,512]{1,0:T(8,128)(2,1)S(1)}, bf16[72,512]{1,0:T(8,128)(2,1)S(1)}, u32[]{:S(2)}, u32[]{:S(2)}) %collective-permute-start.2) | collective-permute-done | bytes 73760 | tf_op jit(solution)/shard_map/ppermute | solution.py:586
  10.6 0.0 copy-start.2
  10.6 0.0 copy-start.3
  10.6 0.0 copy-start.1
  10.6 2.0 %collective-permute-start.3 = (bf16[144,512]{1,0:T(8,128)(2,1)S(1)}, bf16[144,512]{1,0:T(8,128)(2,1)S(1)}, u32[]{:S(2)}, u32[]{:S(2)}) collective-permute-start(bf16[144,512]{1,0:T(8,128)(2,1)S(1)} %hold.5.rest_0_), channel_id=1, source_target_pairs={{0,4},{2,6},{4,0},{6,2},{8,12},{10,14},{12,8},{14,10},{1,5},{3,7},... | collective-permute-start | bytes 442376 | tf_op jit(solution)/shard_map/ppermute | solution.py:592
  12.6 0.2 collective-permute-start.5
  12.8 3.1 %collective-permute-start.8 = (bf16[144,512]{1,0:T(8,128)(2,1)S(1)}, bf16[144,512]{1,0:T(8,128)(2,1)S(1)}, u32[]{:S(2)}, u32[]{:S(2)}) collective-permute-start(bf16[144,512]{1,0:T(8,128)(2,1)S(1)} %hold.5.rest_0_), channel_id=1, source_target_pairs={{0,1},{1,0},{2,3},{3,2},{4,5},{5,4},{6,7},{7,6},{8,9},{9,8},{10,11... | collective-permute-start | bytes 442376 | tf_op jit(solution)/shard_map/ppermute | solution.py:594
  15.8 2.4 %absorb.3.query = bf16[32,128,576]{2,1,0:T(8,128)(2,1)S(1)} custom-call(bf16[128,32,128]{2,1,0:T(8,128)(2,1)} %bitcast.9, bf16[128,2048]{1,0:T(8,128)(2,1)} %bitcast.11, bf16[32,512,128]{2,1,0:T(8,128)(2,1)} %up_ref.3, bf16[32,128,576]{2,1,0:T(8,128)(2,1)S(1)} %absorb.2.rest_0_), custom_call_target="tpu_custom_call", output_to_operand_aliasing={{}: (3, {})} | custom-call | flops 268435456 | bytes 5242880 | tf_op jit(solution)/shard_map/absorb/pallas_call | solution.py:59
  18.2 0.0 collective-permute-done.3.rest_1_
  18.2 1.3 %collective-permute-start.7 = (bf16[144,512]{1,0:T(8,128)(2,1)S(1)}, bf16[144,512]{1,0:T(8,128)(2,1)S(1)}, u32[]{:S(2)}, u32[]{:S(2)}) collective-permute-start(bf16[144,512]{1,0:T(8,128)(2,1)S(1)} %collective-permute-done.3.rest_1_), channel_id=1, source_target_pairs={{0,2},{2,0},{4,6},{6,4},{8,10},{10,8},{12,14},{14,12},{1,3},{3,1},... | collective-permute-start | bytes 442376 | tf_op jit(solution)/shard_map/ppermute | solution.py:596
  19.5 0.9 %collective-permute-start.4 = (bf16[144,512]{1,0:T(8,128)(2,1)S(1)}, bf16[144,512]{1,0:T(8,128)(2,1)S(1)}, u32[]{:S(2)}, u32[]{:S(2)}) collective-permute-start(bf16[144,512]{1,0:T(8,128)(2,1)S(1)} %collective-permute-done.3.rest_1_), channel_id=1, source_target_pairs={{0,1},{1,0},{2,3},{3,2},{4,5},{5,4},{6,7},{7,6},{8,9},{9,8},{10,11... | collective-permute-start | bytes 442376 | tf_op jit(solution)/shard_map/ppermute | solution.py:597
  20.5 0.0 collective-permute-done.5.rest_2_
  20.5 0.5 %collective-permute-start.6 = (bf16[144,512]{1,0:T(8,128)(2,1)S(1)}, bf16[144,512]{1,0:T(8,128)(2,1)S(1)}, u32[]{:S(2)}, u32[]{:S(2)}) collective-permute-start(bf16[144,512]{1,0:T(8,128)(2,1)S(1)} %collective-permute-done.5.rest_2_), channel_id=1, source_target_pairs={{0,1},{1,0},{2,3},{3,2},{4,5},{5,4},{6,7},{7,6},{8,9},{9,8},{10,11... | collective-permute-start | bytes 442376 | tf_op jit(solution)/shard_map/ppermute | solution.py:598
  21.0 0.0 collective-permute-done.8.rest_3_
  21.0 0.0 copy-done.2
  21.0 0.0 copy-done.3
  21.0 2.1 %early.1 = (bf16[1792,576]{1,0:T(8,128)(2,1)S(1)}, f32[4,768,128]{2,1,0:T(8,128)S(1)}, s32[20]{0:T(128)S(1)}) custom-call(s32[4]{0:T(128)S(1)} %copy-done.2, s32[32]{0:T(128)S(1)} %copy-done.3, bf16[144,512]{1,0:T(8,128)(2,1)S(1)} %hold.5.rest_0_, bf16[144,512]{1,0:T(8,128)(2,1)S(1)} %collective-permute-done.3.rest_1_, ...), custom_call_target="tpu_custom_call" | custom-call | tf_op jit(solution)/shard_map/early/pallas_call | solution.py:445
  23.1 0.0 collective-permute-done.7.rest_2_
  23.1 1.4 %collective-permute-start.9 = (bf16[144,512]{1,0:T(8,128)(2,1)S(1)}, bf16[144,512]{1,0:T(8,128)(2,1)S(1)}, u32[]{:S(2)}, u32[]{:S(2)}) collective-permute-start(bf16[144,512]{1,0:T(8,128)(2,1)S(1)} %collective-permute-done.7.rest_2_), channel_id=1, source_target_pairs={{0,1},{1,0},{2,3},{3,2},{4,5},{5,4},{6,7},{7,6},{8,9},{9,8},{10,11... | collective-permute-start | bytes 442376 | tf_op jit(solution)/shard_map/ppermute | solution.py:605
  24.6 0.0 collective-permute-done.4.rest_0_
  24.6 0.0 collective-permute-done.6.rest_1_
  24.6 1.0 %collective-permute-done.9.rest_3_ = bf16[144,512]{1,0:T(8,128)(2,1)S(1)} collective-permute-done((bf16[144,512]{1,0:T(8,128)(2,1)S(1)}, bf16[144,512]{1,0:T(8,128)(2,1)S(1)}, u32[]{:S(2)}, u32[]{:S(2)}) %collective-permute-start.9) | collective-permute-done | bytes 147488 | tf_op jit(solution)/shard_map/ppermute | solution.py:605
  25.6 0.0 copy-done.1
  25.6 13.1 %attend.1 = bf16[128,32,128]{2,1,0:T(8,128)(2,1)} custom-call(bf16[32,128,576]{2,1,0:T(8,128)(2,1)S(1)} %absorb.3.query, bf16[32,512,128]{2,1,0:T(8,128)(2,1)} %value_up_hbm.1, bf16[144,512]{1,0:T(8,128)(2,1)S(1)} %collective-permute-done.4.rest_0_, bf16[144,512]{1,0:T(8,128)(2,1)S(1)} %collective-permute-done.6.rest_1_, ...), custom_call_target="tpu_custom_call" | custom-call | flops 6039797760 | bytes 9961472 | tf_op jit(solution)/shard_map/attend/pallas_call | solution.py:488
  (3 shorter events, 0.0 us)
Async XLA Ops:
  0.0 6.3 %collective-permute-start = (bf16[64,576]{1,0:T(8,128)(2,1)}, bf16[64,576]{1,0:T(8,128)(2,1)S(1)}, u32[]{:S(2)}, u32[]{:S(2)}) collective-permute-start(bf16[64,576]{1,0:T(8,128)(2,1)} %bitcast.4), channel_id=1, source_target_pairs={{0,18},{2,16},{4,22},{6,20},{8,26},{10,24},{12,30},{14,28},{1,19},... | collective-permute-start | bytes 221192 | tf_op jit(solution)/shard_map/ppermute | solution.py:573
  1.3 5.0 %collective-permute-start.1 = (bf16[64,576]{1,0:T(8,128)(2,1)}, bf16[64,576]{1,0:T(8,128)(2,1)S(1)}, u32[]{:S(2)}, u32[]{:S(2)}) collective-permute-start(bf16[64,576]{1,0:T(8,128)(2,1)} %bitcast.5), channel_id=1, source_target_pairs={{0,1},{1,0},{2,3},{3,2},{4,5},{5,4},{6,7},{7,6},{8,9},{9,8},{10,11... | collective-permute-start | bytes 221192 | tf_op jit(solution)/shard_map/ppermute | solution.py:576
  2.0 0.9 %copy-start = (bf16[1,64,576]{2,1,0:T(8,128)(2,1)S(1)}, bf16[1,64,576]{2,1,0:T(8,128)(2,1)}, u32[]{:S(2)}) copy-start(bf16[1,64,576]{2,1,0:T(8,128)(2,1)} %param.9) | copy-start | bytes 221188
  6.4 4.2 %collective-permute-start.2 = (bf16[72,512]{1,0:T(8,128)(2,1)S(1)}, bf16[72,512]{1,0:T(8,128)(2,1)S(1)}, u32[]{:S(2)}, u32[]{:S(2)}) collective-permute-start(bf16[72,512]{1,0:T(8,128)(2,1)S(1)} %hold.4.first), channel_id=1, source_target_pairs={{0,8},{2,10},{4,12},{6,14},{8,0},{10,2},{12,4},{14,6},{1,9},{3,11}... | collective-permute-start | bytes 221192 | tf_op jit(solution)/shard_map/ppermute | solution.py:586
  10.6 10.4 %copy-start.2 = (s32[4]{0:T(128)S(1)}, s32[4]{0:T(128)}, u32[]{:S(2)}) copy-start(s32[4]{0:T(128)} %lengths_ref.1) | copy-start | bytes 52
  10.6 10.4 %copy-start.3 = (s32[32]{0:T(128)S(1)}, s32[32]{0:T(128)}, u32[]{:S(2)}) copy-start(s32[32]{0:T(128)} %table_ref.1) | copy-start | bytes 388
  10.6 15.0 %copy-start.1 = (bf16[1,64,576]{2,1,0:T(8,128)(2,1)S(1)}, bf16[1,64,576]{2,1,0:T(8,128)(2,1)}, u32[]{:S(2)}) copy-start(bf16[1,64,576]{2,1,0:T(8,128)(2,1)} %param.9) | copy-start | bytes 221188
  10.6 7.6 %collective-permute-start.3 = (bf16[144,512]{1,0:T(8,128)(2,1)S(1)}, bf16[144,512]{1,0:T(8,128)(2,1)S(1)}, u32[]{:S(2)}, u32[]{:S(2)}) collective-permute-start(bf16[144,512]{1,0:T(8,128)(2,1)S(1)} %hold.5.rest_0_), channel_id=1, source_target_pairs={{0,4},{2,6},{4,0},{6,2},{8,12},{10,14},{12,8},{14,10},{1,5},{3,7},... | collective-permute-start | bytes 442376 | tf_op jit(solution)/shard_map/ppermute | solution.py:592
  12.6 7.9 %collective-permute-start.5 = (bf16[144,512]{1,0:T(8,128)(2,1)S(1)}, bf16[144,512]{1,0:T(8,128)(2,1)S(1)}, u32[]{:S(2)}, u32[]{:S(2)}) collective-permute-start(bf16[144,512]{1,0:T(8,128)(2,1)S(1)} %hold.5.rest_0_), channel_id=1, source_target_pairs={{0,16},{16,0},{1,17},{17,1},{2,18},{18,2},{3,19},{19,3},{4,20},{20... | collective-permute-start | bytes 442376 | tf_op jit(solution)/shard_map/ppermute | solution.py:593
  12.8 8.2 %collective-permute-start.8 = (bf16[144,512]{1,0:T(8,128)(2,1)S(1)}, bf16[144,512]{1,0:T(8,128)(2,1)S(1)}, u32[]{:S(2)}, u32[]{:S(2)}) collective-permute-start(bf16[144,512]{1,0:T(8,128)(2,1)S(1)} %hold.5.rest_0_), channel_id=1, source_target_pairs={{0,1},{1,0},{2,3},{3,2},{4,5},{5,4},{6,7},{7,6},{8,9},{9,8},{10,11... | collective-permute-start | bytes 442376 | tf_op jit(solution)/shard_map/ppermute | solution.py:594
  18.2 4.9 %collective-permute-start.7 = (bf16[144,512]{1,0:T(8,128)(2,1)S(1)}, bf16[144,512]{1,0:T(8,128)(2,1)S(1)}, u32[]{:S(2)}, u32[]{:S(2)}) collective-permute-start(bf16[144,512]{1,0:T(8,128)(2,1)S(1)} %collective-permute-done.3.rest_1_), channel_id=1, source_target_pairs={{0,2},{2,0},{4,6},{6,4},{8,10},{10,8},{12,14},{14,12},{1,3},{3,1},... | collective-permute-start | bytes 442376 | tf_op jit(solution)/shard_map/ppermute | solution.py:596
  19.5 5.0 %collective-permute-start.4 = (bf16[144,512]{1,0:T(8,128)(2,1)S(1)}, bf16[144,512]{1,0:T(8,128)(2,1)S(1)}, u32[]{:S(2)}, u32[]{:S(2)}) collective-permute-start(bf16[144,512]{1,0:T(8,128)(2,1)S(1)} %collective-permute-done.3.rest_1_), channel_id=1, source_target_pairs={{0,1},{1,0},{2,3},{3,2},{4,5},{5,4},{6,7},{7,6},{8,9},{9,8},{10,11... | collective-permute-start | bytes 442376 | tf_op jit(solution)/shard_map/ppermute | solution.py:597
  20.5 4.1 %collective-permute-start.6 = (bf16[144,512]{1,0:T(8,128)(2,1)S(1)}, bf16[144,512]{1,0:T(8,128)(2,1)S(1)}, u32[]{:S(2)}, u32[]{:S(2)}) collective-permute-start(bf16[144,512]{1,0:T(8,128)(2,1)S(1)} %collective-permute-done.5.rest_2_), channel_id=1, source_target_pairs={{0,1},{1,0},{2,3},{3,2},{4,5},{5,4},{6,7},{7,6},{8,9},{9,8},{10,11... | collective-permute-start | bytes 442376 | tf_op jit(solution)/shard_map/ppermute | solution.py:598
  23.1 2.4 %collective-permute-start.9 = (bf16[144,512]{1,0:T(8,128)(2,1)S(1)}, bf16[144,512]{1,0:T(8,128)(2,1)S(1)}, u32[]{:S(2)}, u32[]{:S(2)}) collective-permute-start(bf16[144,512]{1,0:T(8,128)(2,1)S(1)} %collective-permute-done.7.rest_2_), channel_id=1, source_target_pairs={{0,1},{1,0},{2,3},{3,2},{4,5},{5,4},{6,7},{7,6},{8,9},{9,8},{10,11... | collective-permute-start | bytes 442376 | tf_op jit(solution)/shard_map/ppermute | solution.py:605
